TPU v7x, 768 devices: a whole 4x8x12 slice. The times are simulated.
768 devices in a mesh: grp: 12 (over z), loc: 64 (over x, y, core).
Axes of the slice: x: 4, y: 8, z: 12, core: 2. Of those that a mesh axis runs over, the one named last changes fastest.
Arguments:
- table: float32 [196608, 512], P(('grp', 'loc')), may hold values from -6 to 6
- projection_weight: bfloat16 [512, 2048], replicated, may hold values from -0.25 to 0.25
- output_weight: bfloat16 [512, 512], replicated, may hold values from -0.25 to 0.25
- offsets: int32 [768, 768, 2], P(('grp', 'loc')), may hold values from 0 to 255, as said below
- events: int32 [1536, 176], P(('grp', 'loc')), may hold values from 0 to 1535, as said below
- cotangent: bfloat16 [1536, 176, 512], P(('grp', 'loc')), may hold values from -6 to 6
Outputs:
- layer_out: bfloat16 [1536, 176, 512], P(('grp', 'loc'))
- table_grad: float32 [196608, 512], P(('grp', 'loc'))
Inputs may be any that keep to these rules, and one draw needn't show every extreme that they name: Within one device's block for one owner, the 2 offsets differ. For each device, exactly 96 owners have 2 live slots and 144 have 1 live slot (slot c of owner o is live if c is below that owner's count); owners 0 and 767 always have 2 live slots; events name only live slots o * 2 + c of the device's own list, and every live slot is named by at least one event of the device.
All inputs are finite; a program needn't handle non-finite values.
Results may differ from a plain program's by a relative error of at most 0.015.
Values may be sent and summed in bfloat16 or wider, within the bound.
A program may use at most 32 MiB of HBM per device.

v0:
```python
import jax
import jax.numpy as jnp
from jax import lax
from jax.sharding import PartitionSpec as P

HEADS = 4
LEN = 176


def normalize(values):
    center = values - jnp.mean(values, axis=-1, keepdims=True)
    spread = jnp.mean(center * center, axis=-1, keepdims=True)
    return center * lax.rsqrt(spread + 1e-05)


def hstu_layer(input_rows, projection_weight, output_weight):
    width = input_rows.shape[-1]
    length = input_rows.shape[1]
    normed_rows = normalize(input_rows).astype(jnp.bfloat16)
    branch_parts = jax.nn.silu(
        jnp.einsum(
            "riq,qu->riu", normed_rows, projection_weight, preferred_element_type=jnp.float32
        )
    )
    upper = branch_parts[..., :width].astype(jnp.bfloat16)
    values = branch_parts[..., width : 2 * width].astype(jnp.bfloat16)
    queries = branch_parts[..., 2 * width : 3 * width].astype(jnp.bfloat16)
    keyset = branch_parts[..., 3 * width :].astype(jnp.bfloat16)
    head_dim = width // HEADS
    shape4 = (input_rows.shape[0], length, HEADS, head_dim)
    scores = jnp.einsum(
        "sihd,sjhd->shij",
        queries.reshape(shape4),
        keyset.reshape(shape4),
        preferred_element_type=jnp.float32,
    )
    scores = scores * (1.0 / head_dim**0.5)
    causal = jnp.arange(length)[:, None] >= jnp.arange(length)[None, :]
    weights = jnp.where(causal, jax.nn.silu(scores) / LEN, 0.0).astype(jnp.bfloat16)
    attended = jnp.einsum(
        "shij,sjhd->sihd", weights, values.reshape(shape4), preferred_element_type=jnp.float32
    )
    attended = attended.reshape(input_rows.shape)
    gated_values = (normalize(attended) * upper.astype(jnp.float32)).astype(jnp.bfloat16)
    return input_rows + jnp.einsum(
        "riq,qu->riu", gated_values, output_weight, preferred_element_type=jnp.float32
    )


def local(table, projection_weight, output_weight, offsets, events, cotangent):
    group_count = lax.axis_size("grp")
    local_row_count = lax.axis_size("loc")
    capacity = offsets.shape[-1]
    width = table.shape[-1]
    requests = offsets.reshape(group_count, local_row_count, capacity)
    incoming = lax.all_to_all(
        lax.all_to_all(requests, "grp", split_axis=0, concat_axis=0, tiled=True),
        "loc",
        split_axis=1,
        concat_axis=1,
        tiled=True,
    )
    wanted = incoming.reshape(-1)
    answer_rows = (
        jnp.take(table, wanted, axis=0)
        .astype(jnp.bfloat16)
        .reshape(group_count, local_row_count, capacity, width)
    )
    fetched = lax.all_to_all(
        lax.all_to_all(answer_rows, "grp", split_axis=0, concat_axis=0, tiled=True),
        "loc",
        split_axis=1,
        concat_axis=1,
        tiled=True,
    )
    fetched = lax.optimization_barrier(fetched.reshape(-1, width))
    input_rows = jnp.take(fetched, events, axis=0).astype(jnp.float32)
    output, pullback = jax.vjp(
        lambda given: hstu_layer(given, projection_weight, output_weight), input_rows
    )
    input_grad = pullback(cotangent.astype(jnp.float32))[0]
    slot_grad = (
        jnp.zeros((fetched.shape[0], width), jnp.float32)
        .at[events.reshape(-1)]
        .add(input_grad.reshape(-1, width))
    )
    outgoing = slot_grad.astype(jnp.bfloat16).reshape(group_count, local_row_count, capacity, width)
    returned = lax.all_to_all(
        lax.all_to_all(outgoing, "grp", split_axis=0, concat_axis=0, tiled=True),
        "loc",
        split_axis=1,
        concat_axis=1,
        tiled=True,
    )
    table_grad = (
        jnp.zeros(table.shape, jnp.float32)
        .at[wanted]
        .add(returned.reshape(-1, width).astype(jnp.float32))
    )
    return (output.astype(jnp.bfloat16), table_grad)


def solution(mesh):
    placed = (
        P(("grp", "loc"), None),
        P(),
        P(),
        P(("grp", "loc"), None, None),
        P(("grp", "loc"), None),
        P(("grp", "loc"), None, None),
    )
    return jax.shard_map(
        local,
        mesh=mesh,
        in_specs=placed,
        out_specs=(P(("grp", "loc"), None, None), P(("grp", "loc"), None)),
        check_vma=False,
    )
```

profile of v0, /device:TPU:1, one launch (start us, length us, event | category | flops | bytes accessed | tf_op | source)
XLA Modules:
  0.0 336.1 jit_solution(1494141448752701382)
XLA Ops:
  1.7 24.4 %all_to_all.30 = s32[12,1,128]{2,1,0:T(1,128)S(1)} all-to-all(s32[12,1,128]{2,1,0:T(1,128)S(1)} %reshape.224), channel_id=1, replica_groups=mesh['grp'=12,'loc'=64] {'grp'}, dimensions={0} | all-to-all | bytes 12288 | tf_op jit(solution)/shard_map/all_to_all | solution.py:57
  27.5 21.8 %all_to_all.31 = s32[12,64,2]{0,2,1:T(2,128)S(1)} all-to-all(s32[12,64,2]{0,2,1:T(2,128)S(1)} %copy.99), channel_id=1, replica_groups=mesh['grp'=12,'loc'=64] {'loc'}, dimensions={1} | all-to-all | bytes 12288 | tf_op jit(solution)/shard_map/all_to_all | solution.py:56
  50.2 4.7 %gather_fusion = bf16[1536,512]{1,0:T(8,128)(2,1)} fusion(f32[256,512]{1,0:T(8,128)S(1)} %copy-done.1, s32[2048]{0:T(1024)S(1)} %pad_clamp_fusion), kind=kCustom, calls=%fused_computation | custom fusion | bytes 3151872 | tf_op jit(solution)/shard_map/jit(_take)/gather | solution.py:65
  54.9 3.6 %gather.11 = bf16[12,64,2,512]{3,2,1,0:T(2,128)(2,1)} reshape(bf16[1536,512]{1,0:T(8,128)(2,1)} %gather_fusion) | data formatting | bytes 3145728 | tf_op jit(solution)/shard_map/jit(_take)/gather | solution.py:65
  59.2 3.3 select_convert_fusion
  62.5 58.8 %all_to_all.32 = bf16[12,64,2,512]{3,2,1,0:T(2,128)(2,1)S(1)} all-to-all(bf16[12,64,2,512]{3,2,1,0:T(2,128)(2,1)S(1)} %select_convert_fusion), channel_id=1, replica_groups=mesh['grp'=12,'loc'=64] {'grp'}, dimensions={0} | all-to-all | bytes 3145728 | tf_op jit(solution)/shard_map/all_to_all | solution.py:70
  121.4 2.2 copy.102
  123.6 7.1 %all-to-all-start.3 = ((bf16[12,64,2,512]{3,2,0,1:T(2,128)(2,1)}), bf16[12,64,2,512]{3,2,0,1:T(2,128)(2,1)}, u32[]{:S(2)}, u32[]{:S(2)}) async-start(bf16[12,64,2,512]{3,2,0,1:T(2,128)(2,1)} %copy.102), calls=%async_computation.3 | async-start | bytes 3145728 | tf_op jit(solution)/shard_map/all_to_all | solution.py:69
  131.0 39.5 %all-to-all-done.3 = bf16[12,64,2,512]{3,2,0,1:T(2,128)(2,1)} async-done(((bf16[12,64,2,512]{3,2,0,1:T(2,128)(2,1)}), bf16[12,64,2,512]{3,2,0,1:T(2,128)(2,1)}, u32[]{:S(2)}, u32[]{:S(2)}) %all-to-all-start.3) | async-done | bytes 1572896 | tf_op jit(solution)/shard_map/all_to_all | solution.py:69
  170.5 3.9 %copy.103 = bf16[12,64,2,512]{3,2,1,0:T(2,128)(2,1)} copy(bf16[12,64,2,512]{3,2,0,1:T(2,128)(2,1)} %all-to-all-done.3) | data formatting | bytes 3145728 | tf_op jit(solution)/shard_map/all_to_all | solution.py:69
  174.4 3.7 %reshape.172 = bf16[1536,512]{1,0:T(8,128)(2,1)} reshape(bf16[12,64,2,512]{3,2,1,0:T(2,128)(2,1)} %copy.103) | data formatting | bytes 3145728 | tf_op jit(solution)/shard_map/reshape | solution.py:76
  178.0 3.7 %gather_fusion.1 = bf16[352,512]{1,0:T(8,128)(2,1)S(1)} fusion(bf16[1536,512]{1,0:T(8,128)(2,1)} %reshape.172, s32[1024]{0:T(1024)S(1)} %pad_clamp_fusion.1), kind=kCustom, calls=%fused_computation.1 | custom fusion | bytes 722304 | tf_op jit(solution)/shard_map/jit(_take)/gather | solution.py:77
  192.3 5.2 %scatter_custom_fusion = f32[1536,512]{1,0:T(8,128)} fusion(s32[352]{0:T(512)S(1)} %fusion.79, f32[352,512]{1,0:T(8,128)} %bitcast.125, f32[]{:T(128)} %constant.60.clone.1), kind=kCustom, calls=%fused_computation.25 | custom fusion | flops 180224 | bytes 3146240 | tf_op jit(solution)/shard_map/scatter-add | solution.py:85
  197.6 3.2 convert_element_type.117
  200.8 3.7 %reshape.180 = bf16[12,64,2,512]{3,2,1,0:T(2,128)(2,1)} reshape(bf16[1536,512]{1,0:T(8,128)(2,1)} %convert_element_type.117) | data formatting | bytes 3145728 | tf_op jit(solution)/shard_map/reshape | solution.py:87
  204.5 60.2 %all_to_all.33 = bf16[12,64,2,512]{3,2,1,0:T(2,128)(2,1)S(1)} all-to-all(bf16[12,64,2,512]{3,2,1,0:T(2,128)(2,1)} %reshape.180), channel_id=1, replica_groups=mesh['grp'=12,'loc'=64] {'grp'}, dimensions={0} | all-to-all | bytes 3145728 | tf_op jit(solution)/shard_map/all_to_all | solution.py:89
  264.6 2.2 copy.117
  266.8 7.2 %all-to-all-start.5 = ((bf16[12,64,2,512]{3,2,0,1:T(2,128)(2,1)}), bf16[12,64,2,512]{3,2,0,1:T(2,128)(2,1)}, u32[]{:S(2)}, u32[]{:S(2)}) async-start(bf16[12,64,2,512]{3,2,0,1:T(2,128)(2,1)} %copy.117), calls=%async_computation.5 | async-start | bytes 3145728 | tf_op jit(solution)/shard_map/all_to_all | solution.py:88
  274.1 2.3 fusion.26
  276.4 37.4 %all-to-all-done.5 = bf16[12,64,2,512]{3,2,0,1:T(2,128)(2,1)} async-done(((bf16[12,64,2,512]{3,2,0,1:T(2,128)(2,1)}), bf16[12,64,2,512]{3,2,0,1:T(2,128)(2,1)}, u32[]{:S(2)}, u32[]{:S(2)}) %all-to-all-start.5) | async-done | bytes 1572896 | tf_op jit(solution)/shard_map/all_to_all | solution.py:88
  313.8 1.9 copy_convert_fusion
  315.7 4.1 %copy.119 = f32[12,64,2,512]{3,2,1,0:T(2,128)} copy(f32[12,64,2,512]{3,1,2,0:T(8,128)S(1)} %copy_convert_fusion) | data formatting | bytes 6291456 | tf_op jit(solution)/shard_map/convert_element_type | solution.py:98
  319.8 5.3 %reshape.210 = f32[1536,512]{1,0:T(8,128)} reshape(f32[12,64,2,512]{3,2,1,0:T(2,128)} %copy.119) | data formatting | bytes 6291456 | tf_op jit(solution)/shard_map/convert_element_type | solution.py:98
  325.1 11.0 %scatter_custom_fusion.1 = f32[256,512]{1,0:T(8,128)} fusion(s32[1536]{0:T(1024)S(1)} %fusion.78, f32[1536,512]{1,0:T(8,128)} %reshape.210, f32[]{:T(128)} %constant.60.clone.1), kind=kCustom, calls=%fused_computation.105 | custom fusion | flops 786432 | bytes 524800 | tf_op jit(solution)/shard_map/scatter-add | solution.py:98
  (58 shorter events, 14.7 us)
Async XLA Ops:
  0.6 181.7 %copy-start = (bf16[512,2048]{1,0:T(8,128)(2,1)S(1)}, bf16[512,2048]{1,0:T(8,128)(2,1)}, u32[]{:S(2)}) copy-start(bf16[512,2048]{1,0:T(8,128)(2,1)} %param.7) | copy-start | bytes 6291460
  0.6 49.5 %copy-start.1 = (f32[256,512]{1,0:T(8,128)S(1)}, f32[256,512]{1,0:T(8,128)}, u32[]{:S(2)}) copy-start(f32[256,512]{1,0:T(8,128)} %param.6) | copy-start | bytes 1572868
  123.6 7.1 %copy-start.5 = (s32[2,176]{1,0:T(2,128)S(1)}, s32[2,176]{1,0:T(2,128)}, u32[]{:S(2)}) copy-start(s32[2,176]{1,0:T(2,128)} %param.10) | copy-start | bytes 4228
  123.6 46.9 %all-to-all-start.3 = ((bf16[12,64,2,512]{3,2,0,1:T(2,128)(2,1)}), bf16[12,64,2,512]{3,2,0,1:T(2,128)(2,1)}, u32[]{:S(2)}, u32[]{:S(2)}) async-start(bf16[12,64,2,512]{3,2,0,1:T(2,128)(2,1)} %copy.102), calls=%async_computation.3 | async-start | bytes 3145728 | tf_op jit(solution)/shard_map/all_to_all | solution.py:69
  183.5 3.1 copy-start.2
  184.5 1.0 copy-start.3
  184.5 1.1 copy-start.4
  266.8 47.0 %all-to-all-start.5 = ((bf16[12,64,2,512]{3,2,0,1:T(2,128)(2,1)}), bf16[12,64,2,512]{3,2,0,1:T(2,128)(2,1)}, u32[]{:S(2)}, u32[]{:S(2)}) async-start(bf16[12,64,2,512]{3,2,0,1:T(2,128)(2,1)} %copy.117), calls=%async_computation.5 | async-start | bytes 3145728 | tf_op jit(solution)/shard_map/all_to_all | solution.py:88
where the time goes:
time: 337 us; the launch traced here: 336 us
  blocking collectives  165 us (49%)
  waiting for transfers between devices  76.9 us (23%)
  local copies, waits for them, and re-layouts  41.1 us (12%)
  other arithmetic  28.9 us (9%)
  starting transfers between devices  14.3 us (4%)
  matrix products  8.76 us (3%)
    all_to_all x1, blocking collectives, local(): lax.all_to_all(outgoing, 'grp', split_axis=0, concat_axis=0, tiled=True)  60.2 us
    all_to_all x1, blocking collectives, local(): lax.all_to_all(answer_rows, 'grp', split_axis=0, concat_axis=0, tiled=True)  58.8 us
    all_to_all x1, waiting for transfers between devices, local(): lax.all_to_all(lax.all_to_all(answer_rows, 'grp', split_axis=0, concat_ax...  39.5 us
    all_to_all x1, waiting for transfers between devices, local(): lax.all_to_all(lax.all_to_all(outgoing, 'grp', split_axis=0, concat_axis=...  37.4 us
    all_to_all x1, blocking collectives, local(): lax.all_to_all(requests, 'grp', split_axis=0, concat_axis=0, tiled=True)  24.4 us
    all_to_all x1, blocking collectives, local(): lax.all_to_all(lax.all_to_all(requests, 'grp', split_axis=0, concat_axis=...  21.8 us
    scatter-add x1, other arithmetic, local(): table_grad = jnp.zeros(table.shape, jnp.float32).at[wanted].add(returned....  11 us
    convert_element_type x2, local copies, waits for them, and re-layouts, local(): returned.reshape(-1, width).astype(jnp.float32)  9.38 us
  transfers between devices with their start and end apart: 2, of which 2 were waited for; matrix products, arithmetic and copies ran while one was open for 1% of the time, Pallas kernels for 0%

commit v1 on v0

v1 whole, which is shorter than its diff:
```python
import functools

import jax
import jax.numpy as jnp
from jax import lax
from jax.experimental import pallas as pl
from jax.experimental.pallas import tpu as pltpu
from jax.sharding import PartitionSpec as P

MESH = pl.DeviceIdType.MESH
F32, BF16 = jnp.float32, jnp.bfloat16
GROUPS, LOCS, CHIPS = 12, 64, 32
ROWS, WIDTH, HEADS, LEN, SEQS = 256, 512, 4, 176, 2
EVENTS = SEQS * LEN
HEAD = WIDTH // HEADS
ORDER = (0, 1, -1, 2, -2, 3, -3, 4, -4, 5, -5, 6)
CHUNKS, PER = 3, 4
MSG = PER * 4
SLOTS = CHIPS * MSG
HALF = ROWS // 2


def place(k):
    return ORDER.index(6 if k == -6 else k)


def parts(hop, side):
    return (0, 1) if hop < 5 else ((0,) if side == 0 else (1,))


def dot(a, b, ca=1, cb=0):
    return lax.dot_general(a, b, (((ca,), (cb,)), ((), ())), preferred_element_type=F32)


def hot(mask):
    return jnp.where(mask, 1.0, 0.0).astype(BF16)


def iota(shape, dim):
    return lax.broadcasted_iota(jnp.int32, shape, dim)


def event_slot(ev, g):
    k = (ev >> 7) - g
    k = jnp.where(k < 0, k + GROUPS, k)
    at = jnp.where(k == 0, 0, jnp.where(k <= 6, 2 * k - 1, 2 * (GROUPS - k)))
    return (at >> 2) * SLOTS + ((ev & 127) >> 2) * MSG + (at & 3) * 4 + (ev & 3)


def lane_of(row, ch, g):
    which = (row & (MSG - 1)) >> 2
    lane = row & 3
    for j in range(PER):
        there = lax.rem(g + ORDER[PER * ch + j] + GROUPS, GROUPS)
        lane = lane + jnp.where(which == j, 4 * there, 0)
    return lane


def norm_stats(x):
    center = x - jnp.mean(x, axis=-1, keepdims=True)
    rstd = lax.rsqrt(jnp.mean(center * center, axis=-1, keepdims=True) + 1e-05)
    return center * rstd, rstd


def norm_back(grad, normed, rstd):
    m1 = jnp.mean(grad, axis=-1, keepdims=True)
    m2 = jnp.mean(grad * normed, axis=-1, keepdims=True)
    return rstd * (grad - m1 - normed * m2)


def kernel(
    table, req, evc, evr, cot_h, wp_h, wo_h, out, tgrad,
    wp, wo, cot, w_sem,
    ag, rq, sb, fet, sg, ret, own, sx_out, sx_in, rs_out, rs_in,
    xhat_s, dsilu, branch, dbranch, att,
    zs, zr, sib_s, sib_r, q_s, q_r, f_s, f_r, b_s, b_r, sx_s, sx_r, rs_s, rs_r,
):
    g, l = lax.axis_index("grp"), lax.axis_index("loc")
    chip, core = lax.div(l, 2), lax.rem(l, 2)
    sib = l + 1 - 2 * core
    nxt = (lax.rem(g + 1, GROUPS), lax.rem(g + GROUPS - 1, GROUPS))

    loads = [
        pltpu.make_async_copy(a, b, w_sem.at[i])
        for i, (a, b) in enumerate(((wp_h, wp), (wo_h, wo), (cot_h, cot)))
    ]
    for load in loads:
        load.start()

    def remote(src, dst, s, r, who):
        return pltpu.make_async_remote_copy(
            src_ref=src, dst_ref=dst, send_sem=s, recv_sem=r, device_id=who, device_id_type=MESH
        )

    bar = pltpu.get_barrier_semaphore()

    def greet(i, _):
        d = lax.rem(chip + i, CHIPS)
        pl.semaphore_signal(bar, inc=1, device_id=(g, 2 * d + core), device_id_type=MESH)
        return 0

    for to in nxt:
        pl.semaphore_signal(bar, inc=1, device_id=(to, l), device_id_type=MESH)
    pl.semaphore_signal(bar, inc=1, device_id=(g, sib), device_id_type=MESH)
    lax.fori_loop(1, CHIPS, greet, 0)
    ag[0, pl.ds(core, 1)] = table[...].astype(BF16)[None]
    rq[pl.ds(chip, 1)] = req[pl.ds(chip, 1)]
    pl.semaphore_wait(bar, CHIPS + 2)

    def ring(side, hop, p):
        sign = -1 if side == 0 else 1
        a, b = place(sign * hop), place(sign * (hop + 1))
        rows = pl.ds(p * HALF, HALF)
        return remote(
            ag.at[a, core, rows], ag.at[b, core, rows], zs.at[side, hop, p], zr.at[side, hop, p], (nxt[side], l)
        )

    def share(at, p):
        rows = pl.ds(p * HALF, HALF)
        return remote(
            ag.at[at, core, rows], ag.at[at, core, rows], sib_s.at[at, p], sib_r.at[at, p], (g, sib)
        )

    for p in range(2):
        ring(0, 0, p).start()
        ring(1, 0, p).start()

    def ask(i, _):
        d = lax.rem(chip + i, CHIPS)
        remote(req.at[d], rq.at[chip], q_s, q_r, (g, 2 * d + core)).start()
        return 0

    lax.fori_loop(1, CHIPS, ask, 0)
    for p in range(2):
        share(0, p).start()

    def spread(src, dst, s, r):
        def one(i, _):
            d = lax.rem(chip + i, CHIPS)
            remote(src.at[d], dst.at[chip], s, r, (g, 2 * d + core)).start()
            return 0

        lax.fori_loop(1, CHIPS, one, 0)
        dst[pl.ds(chip, 1)] = src[pl.ds(chip, 1)]

    def landed(ref, sem):
        view = ref.at[pl.ds(0, CHIPS - 1)]
        pltpu.make_async_copy(view, view, sem).wait()

    def requests():
        return rq[...].reshape(CHIPS, 128).astype(F32).astype(BF16)

    def answer(ch):
        row = iota((SLOTS, 128), 0)
        spread_rows = hot((iota((SLOTS, CHIPS), 0) >> 4) == iota((SLOTS, CHIPS), 1))
        picked = jnp.where(iota((SLOTS, 128), 1) == lane_of(row, ch, g), dot(spread_rows, requests()), 0.0)
        index = dot(picked.astype(BF16), jnp.ones((128, 128), BF16)).astype(jnp.int32)
        target = index + 256 * ((row & (MSG - 1)) >> 1)
        lane = iota((SLOTS, 128), 1)
        pick = jnp.concatenate([hot(target == lane + 128 * b) for b in range(16)], axis=1)
        block = ag[pl.ds(PER * ch, PER)].reshape(PER * 2 * ROWS, WIDTH)
        sb[ch] = dot(pick, block).astype(BF16).reshape(CHIPS, MSG, WIDTH)
        spread(sb.at[ch], fet.at[ch], f_s.at[ch], f_r.at[ch])

    shared = [0]
    for hop in range(6):
        for p in range(2):
            for side in range(2):
                if p in parts(hop, side):
                    at = place((-1 if side == 0 else 1) * (hop + 1))
                    ring(side, hop, p).wait_recv()
                    if hop < 5 and p in parts(hop + 1, side):
                        ring(side, hop + 1, p).start()
                    share(at, p).start()
        if hop % 2 == 1:
            ch = hop // 2
            if ch == 0:
                landed(req, q_s)
                landed(rq, q_r)
            for at in range(PER * ch, PER * ch + PER):
                for p in range(2):
                    share(at, p).wait_recv()
            answer(ch)

    slot_c = event_slot(evc[...], g)
    slot_r = event_slot(evr[...], g)
    x = jnp.zeros((EVENTS, WIDTH), F32)
    for ch in range(CHUNKS):
        landed(fet.at[ch], f_r.at[ch])
        x += dot(hot(slot_c - SLOTS * ch == iota((EVENTS, SLOTS), 1)), fet[ch].reshape(SLOTS, WIDTH))
    for load in loads:
        load.wait()

    xhat, xrstd = norm_stats(x)
    xhat_s[...] = xhat
    normed = xhat.astype(BF16)
    for b in range(4):
        v = dot(normed, wp[:, b * WIDTH : (b + 1) * WIDTH])
        sig = 1.0 / (1.0 + jnp.exp(-v))
        branch[b] = (v * sig).astype(BF16)
        dsilu[b] = sig * (1.0 + v * (1.0 - sig))
    scale = 1.0 / HEAD**0.5
    causal = iota((LEN, LEN), 0) >= iota((LEN, LEN), 1)

    def head(b, s, h):
        return branch[b, s * LEN : (s + 1) * LEN, h * HEAD : (h + 1) * HEAD]

    def weigh(s, h):
        sc = dot(head(2, s, h), head(3, s, h), 1, 1) * scale
        sig = 1.0 / (1.0 + jnp.exp(-sc))
        return jnp.where(causal, sc * sig / LEN, 0.0).astype(BF16), jnp.where(
            causal, sig * (1.0 + sc * (1.0 - sig)), 0.0
        )

    for s in range(SEQS):
        for h in range(HEADS):
            w, _ = weigh(s, h)
            att[s * LEN : (s + 1) * LEN, h * HEAD : (h + 1) * HEAD] = dot(w, head(1, s, h))
    ahat, arstd = norm_stats(att[...])
    upper = branch[0].astype(F32)
    gated = (ahat * upper).astype(BF16)
    out[...] = (x + dot(gated, wo[...])).astype(BF16)

    dgated = dot(cot[...], wo[...], 1, 1).astype(BF16).astype(F32)
    dbranch[0] = ((dgated * ahat).astype(BF16).astype(F32) * dsilu[0]).astype(BF16)
    att[...] = norm_back(dgated * upper, ahat, arstd)
    for s in range(SEQS):
        for h in range(HEADS):
            rows, cols = slice(s * LEN, (s + 1) * LEN), slice(h * HEAD, (h + 1) * HEAD)
            w, slope = weigh(s, h)
            da = att[rows, cols].astype(BF16)
            dw = dot(da, head(1, s, h), 1, 1).astype(BF16).astype(F32)
            dsc = (dw * slope * (scale / LEN)).astype(BF16)
            for b, val in (
                (1, dot(w, da, 0, 0)),
                (2, dot(dsc, head(3, s, h))),
                (3, dot(dsc, head(2, s, h), 0, 0)),
            ):
                dbranch[b, rows, cols] = (
                    val.astype(BF16).astype(F32) * dsilu[b, rows, cols]
                ).astype(BF16)
    dnormed = jnp.zeros((EVENTS, WIDTH), F32)
    for b in range(4):
        dnormed += dot(dbranch[b], wp[:, b * WIDTH : (b + 1) * WIDTH], 1, 1)
    dx = cot[...].astype(F32) + norm_back(dnormed.astype(BF16).astype(F32), xhat_s[...], xrstd)
    high = dx.astype(BF16)
    low = (dx - high.astype(F32)).astype(BF16)
    for ch in reversed(range(CHUNKS)):
        where = hot(slot_r - SLOTS * ch == iota((SLOTS, EVENTS), 0))
        sg[ch] = (dot(where, high) + dot(where, low)).astype(BF16).reshape(CHIPS, MSG, WIDTH)
        spread(sg.at[ch], ret.at[ch], b_s.at[ch], b_r.at[ch])

    def swap(at):
        return remote(sx_out.at[at], sx_in.at[at], sx_s.at[at], sx_r.at[at], (g, sib))

    def collect(ch):
        landed(ret.at[ch], b_r.at[ch])
        lane, col = iota((128, SLOTS), 0), iota((128, SLOTS), 1)
        sel = dot(requests(), hot(lane == lane_of(col, ch, g)))
        mine = (iota((CHIPS, SLOTS), 1) >> 4) == iota((CHIPS, SLOTS), 0)
        index = dot(jnp.ones((8, CHIPS), BF16), jnp.where(mine, sel, 0.0).astype(BF16))[0:1].astype(jnp.int32)
        kind = (iota((1, SLOTS), 1) & (MSG - 1)) >> 1
        row = iota((ROWS, SLOTS), 0)
        grads = ret[ch].reshape(SLOTS, WIDTH)
        for j in reversed(range(PER)):
            at = PER * ch + j
            for other in (True, False):
                col_core = 1 - core if other else core
                mine = jnp.where(kind == 2 * j + col_core, index, -1)
                total = dot(hot(row == mine), grads)
                if other:
                    sx_out[at] = total.astype(BF16)
                    swap(at).start()
                else:
                    own[at] = total

    def pass_on(side, s, p):
        rows = pl.ds(p * HALF, HALF)
        return remote(
            rs_out.at[side, s - 1, rows], rs_in.at[side, s - 1, rows],
            rs_s.at[side, 6 - s, p], rs_r.at[side, 6 - s, p], (nxt[side], l),
        )

    done, got = [], []
    for s in range(6, -1, -1):
        for side in range(2):
            at = place(s if side == 0 else -s)
            if at // PER not in done:
                collect(at // PER)
                done.append(at // PER)
            if at not in got:
                swap(at).wait_recv()
                got.append(at)
            if s == 0:
                continue
            for p in ((0, 1) if s < 6 else (side,)):
                rows = slice(p * HALF, (p + 1) * HALF)
                total = own[at, rows] + sx_in[at, rows].astype(F32)
                if s < 5 or (s == 5 and p == side):
                    pass_on(side, s + 1, p).wait_recv()
                    total += rs_in[side, s, rows].astype(F32)
                rs_out[side, s - 1, rows] = total.astype(BF16)
                pass_on(side, s, p).start()
    for p in range(2):
        rows = slice(p * HALF, (p + 1) * HALF)
        total = own[0, rows] + sx_in[0, rows].astype(F32)
        for side in range(2):
            pass_on(side, 1, p).wait_recv()
            total += rs_in[side, 0, rows].astype(F32)
        tgrad[rows] = total

    for side in range(2):
        for hop in range(6):
            for p in parts(hop, side):
                ring(side, hop, p).wait_send()
        for s in range(1, 7):
            for p in ((0, 1) if s < 6 else (side,)):
                pass_on(side, s, p).wait_send()
    for at in range(GROUPS):
        for p in range(2):
            share(at, p).wait_send()
        swap(at).wait_send()
    for ch in range(CHUNKS):
        landed(sb.at[ch], f_s.at[ch])
        landed(sg.at[ch], b_s.at[ch])


def local(table, projection_weight, output_weight, offsets, events, cotangent):
    asked = offsets.reshape(GROUPS, CHIPS, 4).transpose(1, 0, 2).reshape(CHIPS, 1, 4 * GROUPS)
    asked = jnp.pad(asked, ((0, 0), (0, 0), (0, 128 - 4 * GROUPS)))
    vmem, anym = pl.BlockSpec(memory_space=pltpu.VMEM), pl.BlockSpec(memory_space=pl.ANY)
    dma = pltpu.SemaphoreType.DMA
    out, grad = pl.pallas_call(
        kernel,
        out_shape=(
            jax.ShapeDtypeStruct((EVENTS, WIDTH), BF16),
            jax.ShapeDtypeStruct((ROWS, WIDTH), F32),
        ),
        in_specs=[vmem] * 4 + [anym] * 3,
        out_specs=(vmem, vmem),
        scratch_shapes=[
            pltpu.VMEM((WIDTH, 4 * WIDTH), BF16),
            pltpu.VMEM((WIDTH, WIDTH), BF16),
            pltpu.VMEM((EVENTS, WIDTH), BF16),
            dma((3,)),
            pltpu.VMEM((GROUPS, 2, ROWS, WIDTH), BF16),
            pltpu.VMEM((CHIPS, 1, 128), jnp.int32),
            pltpu.VMEM((CHUNKS, CHIPS, MSG, WIDTH), BF16),
            pltpu.VMEM((CHUNKS, CHIPS, MSG, WIDTH), BF16),
            pltpu.VMEM((CHUNKS, CHIPS, MSG, WIDTH), BF16),
            pltpu.VMEM((CHUNKS, CHIPS, MSG, WIDTH), BF16),
            pltpu.VMEM((GROUPS, ROWS, WIDTH), F32),
            pltpu.VMEM((GROUPS, ROWS, WIDTH), BF16),
            pltpu.VMEM((GROUPS, ROWS, WIDTH), BF16),
            pltpu.VMEM((2, 6, ROWS, WIDTH), BF16),
            pltpu.VMEM((2, 6, ROWS, WIDTH), BF16),
            pltpu.VMEM((EVENTS, WIDTH), F32),
            pltpu.VMEM((4, EVENTS, WIDTH), F32),
            pltpu.VMEM((4, EVENTS, WIDTH), BF16),
            pltpu.VMEM((4, EVENTS, WIDTH), BF16),
            pltpu.VMEM((EVENTS, WIDTH), F32),
            dma((2, 6, 2)), dma((2, 6, 2)), dma((GROUPS, 2)), dma((GROUPS, 2)),
            dma, dma, dma((CHUNKS,)), dma((CHUNKS,)), dma((CHUNKS,)), dma((CHUNKS,)),
            dma((GROUPS,)), dma((GROUPS,)), dma((2, 6, 2)), dma((2, 6, 2)),
        ],
        compiler_params=pltpu.CompilerParams(
            collective_id=0, has_side_effects=True, vmem_limit_bytes=60 << 20
        ),
    )(
        table,
        asked,
        events.reshape(EVENTS, 1),
        events.reshape(1, EVENTS),
        cotangent.reshape(EVENTS, WIDTH),
        projection_weight,
        output_weight,
    )
    return out.reshape(cotangent.shape), grad


def solution(mesh):
    placed = (
        P(("grp", "loc"), None),
        P(),
        P(),
        P(("grp", "loc"), None, None),
        P(("grp", "loc"), None),
        P(("grp", "loc"), None, None),
    )
    return jax.shard_map(
        local,
        mesh=mesh,
        in_specs=placed,
        out_specs=(P(("grp", "loc"), None, None), P(("grp", "loc"), None)),
        check_vma=False,
    )
```

time: 337 us -> 151 us (0.45)
  blocking collectives: 165 us -> 0 us
  Pallas kernels: 0 us -> 142 us
  waiting for transfers between devices: 76.9 us -> 0 us
  local copies, waits for them, and re-layouts: 41.1 us -> 8.34 us
  other arithmetic: 28.9 us -> 0 us
  starting transfers between devices: 14.3 us -> 0 us
  matrix products: 8.76 us -> 0 us
    all_to_all x4 -> x0, blocking collectives: 165 us -> none  [the longest x1 60.2 us: local(): lax.all_to_all(outgoing, 'grp', split_axis=0, concat_axis=0, tiled=True)]
    pallas_call x0 -> x1, Pallas kernels: none -> 142 us  [local(): pl.pallas_call(kernel, out_shape=(jax.ShapeDtypeStruct((EVENTS, WIDTH), B...]
    all_to_all x2 -> x0, waiting for transfers between devices: 76.9 us -> none  [the longest x1 39.5 us: local(): lax.all_to_all(lax.all_to_all(answer_rows, 'grp', split_axis=0, concat_ax...]
    scatter-add x2 -> x0, other arithmetic: 16.3 us -> none  [the longest x1 11 us: local(): table_grad = jnp.zeros(table.shape, jnp.float32).at[wanted].add(returned....]
    all_to_all x2 -> x0, starting transfers between devices: 14.3 us -> none  [the longest x1 7.23 us: local(): lax.all_to_all(lax.all_to_all(outgoing, 'grp', split_axis=0, concat_axis=...]
    gather x3 -> x0, local copies, waits for them, and re-layouts: 12 us -> none  [the longest x2 8.33 us: local(): jnp.take(table, wanted, axis=0).astype(jnp.bfloat16)]
    all_to_all x6 -> x0, local copies, waits for them, and re-layouts: 9.56 us -> none  [the longest x1 3.9 us: local(): lax.all_to_all(lax.all_to_all(answer_rows, 'grp', split_axis=0, concat_ax...]
    convert_element_type x4 -> x0, local copies, waits for them, and re-layouts: 9.5 us -> none  [the longest x2 9.38 us: local(): returned.reshape(-1, width).astype(jnp.float32)]
  transfers between devices with their start and end apart: 2 -> 0, of which waited for: 2 -> 0; matrix products, arithmetic and copies ran while one was open for 1% -> 0% of each run, Pallas kernels for 0% -> 0%
where the time goes in v1:
time: 151 us
  Pallas kernels  142 us (94%)
  local copies, waits for them, and re-layouts  8.34 us (6%)
    pallas_call x1, Pallas kernels, local(): pl.pallas_call(kernel, out_shape=(jax.ShapeDtypeStruct((EVENTS, WIDTH), B...  142 us
    unnamed x3, local copies, waits for them, and re-layouts  4.48 us

profile of v1, /device:TPU:1, one launch (start us, length us, event | category | flops | bytes accessed | tf_op | source)
XLA Modules:
  0.0 150.7 jit_solution(15845593109783465813)
XLA Ops:
  0.6 1.3 reshape.25.evr
  2.0 1.6 %reshape.28.evc = s32[352,1]{1,0:T(8,128)} reshape(s32[2,176]{1,0:T(2,128)} %param.10) | data formatting | bytes 2816 | tf_op jit(solution)/shard_map/reshape | solution.py:372
  3.5 0.9 copy.8
  4.4 0.1 reshape.22
  4.5 0.1 copy.9
  4.7 0.1 copy.10
  4.7 0.6 pad.4.req
  5.4 141.7 %shard_map.77 = (bf16[352,512]{1,0:T(8,128)(2,1)}, f32[256,512]{1,0:T(8,128)}) custom-call(f32[256,512]{1,0:T(8,128)} %table.1, s32[32,1,128]{2,1,0:T(1,128)} %pad.4.req, s32[352,1]{1,0:T(8,128)} %reshape.28.evc, s32[1,352]{1,0:T(1,128)} %reshape.25.evr, bf16[352,512]{1,0:T(8,128)(2,1)} %bitcast.5, bf16[512,2048]{1,0:T(8,128)(2,1)} %wp_h.1, ...), custom_call_target="tpu_custom_call" | custom-call | tf_op jit(solution)/shard_map/pallas_call | solution.py:333
  147.0 1.7 %copy.14 = bf16[2,176,512]{2,1,0:T(8,128)(2,1)} copy(bf16[2,176,512]{2,1,0:T(8,128)(2,1)} %bitcast.6) | data formatting | bytes 720896
  148.8 1.9 %copy.15 = f32[256,512]{1,0:T(8,128)} copy(f32[256,512]{1,0:T(8,128)} %get-tuple-element.9) | data formatting | bytes 1048576

commit v2 on v1

--- a/solution.py
+++ b/solution.py
@@ -14,9 +14,10 @@
 EVENTS = SEQS * LEN
 HEAD = WIDTH // HEADS
 ORDER = (0, 1, -1, 2, -2, 3, -3, 4, -4, 5, -5, 6)
-CHUNKS, PER = 3, 4
+CHUNKS, PER = 6, 2
 MSG = PER * 4
 SLOTS = CHIPS * MSG
+SIDE = WIDTH // 2
 HALF = ROWS // 2
 
 
@@ -44,7 +45,7 @@
     k = (ev >> 7) - g
     k = jnp.where(k < 0, k + GROUPS, k)
     at = jnp.where(k == 0, 0, jnp.where(k <= 6, 2 * k - 1, 2 * (GROUPS - k)))
-    return (at >> 2) * SLOTS + ((ev & 127) >> 2) * MSG + (at & 3) * 4 + (ev & 3)
+    return (at >> 1) * SLOTS + ((ev & 127) >> 2) * MSG + (at & 1) * 4 + (ev & 3)
 
 
 def lane_of(row, ch, g):
@@ -56,6 +57,17 @@
     return lane
 
 
+def stack(x):
+    x = x.astype(BF16).astype(F32).reshape(CHIPS, MSG, WIDTH)
+    return jnp.concatenate([x[:, :, :SIDE], x[:, :, SIDE:]], axis=1).astype(BF16)
+
+
+def unstack(x):
+    x = x.astype(F32)
+    x = jnp.concatenate([x[:, :MSG], x[:, MSG:]], axis=2)
+    return x.reshape(SLOTS, WIDTH).astype(BF16)
+
+
 def norm_stats(x):
     center = x - jnp.mean(x, axis=-1, keepdims=True)
     rstd = lax.rsqrt(jnp.mean(center * center, axis=-1, keepdims=True) + 1e-05)
@@ -69,9 +81,9 @@
 
 
 def kernel(
-    table, req, evc, evr, cot_h, wp_h, wo_h, out, tgrad,
-    wp, wo, cot, w_sem,
-    ag, rq, sb, fet, sg, ret, own, sx_out, sx_in, rs_out, rs_in,
+    table_h, offs, evs, cot_h, wp_h, wo_h, out, tgrad,
+    table, wp, wo, cot, w_sem,
+    ag, req, rq, sb, fet, sg, ret, own, sx_out, sx_in, rs_out, rs_in,
     xhat_s, dsilu, branch, dbranch, att,
     zs, zr, sib_s, sib_r, q_s, q_r, f_s, f_r, b_s, b_r, sx_s, sx_r, rs_s, rs_r,
 ):
@@ -82,7 +94,7 @@
 
     loads = [
         pltpu.make_async_copy(a, b, w_sem.at[i])
-        for i, (a, b) in enumerate(((wp_h, wp), (wo_h, wo), (cot_h, cot)))
+        for i, (a, b) in enumerate(((table_h, table), (wp_h, wp), (wo_h, wo), (cot_h, cot)))
     ]
     for load in loads:
         load.start()
@@ -103,6 +115,14 @@
         pl.semaphore_signal(bar, inc=1, device_id=(to, l), device_id_type=MESH)
     pl.semaphore_signal(bar, inc=1, device_id=(g, sib), device_id_type=MESH)
     lax.fori_loop(1, CHIPS, greet, 0)
+    owner, lane = iota((WIDTH + SIDE, 128), 0), iota((WIDTH + SIDE, 128), 1)
+    asks = jnp.zeros((CHIPS, 128), F32)
+    of_chip = (iota((CHIPS, WIDTH + SIDE), 1) & (LOCS - 1)) >> 1 == iota((CHIPS, WIDTH + SIDE), 0)
+    for slot in range(2):
+        picked = jnp.where(of_chip, offs[slot : slot + 1].astype(F32), 0.0).astype(BF16)
+        asks += dot(picked, hot(lane == (owner >> 6) * 4 + (owner & 1) * 2 + slot))
+    req[...] = asks.reshape(CHIPS, 1, 128)
+    loads[0].wait()
     ag[0, pl.ds(core, 1)] = table[...].astype(BF16)[None]
     rq[pl.ds(chip, 1)] = req[pl.ds(chip, 1)]
     pl.semaphore_wait(bar, CHIPS + 2)
@@ -134,35 +154,42 @@
     for p in range(2):
         share(0, p).start()
 
-    def spread(src, dst, s, r):
+    def spread(src, dst, s, r, first=1, last=CHIPS):
         def one(i, _):
             d = lax.rem(chip + i, CHIPS)
             remote(src.at[d], dst.at[chip], s, r, (g, 2 * d + core)).start()
             return 0
 
-        lax.fori_loop(1, CHIPS, one, 0)
-        dst[pl.ds(chip, 1)] = src[pl.ds(chip, 1)]
+        lax.fori_loop(first, last, one, 0)
+        if last == CHIPS:
+            dst[pl.ds(chip, 1)] = src[pl.ds(chip, 1)]
 
     def landed(ref, sem):
         view = ref.at[pl.ds(0, CHIPS - 1)]
         pltpu.make_async_copy(view, view, sem).wait()
 
     def requests():
-        return rq[...].reshape(CHIPS, 128).astype(F32).astype(BF16)
+        return rq[...].reshape(CHIPS, 128).astype(BF16)
 
     def answer(ch):
         row = iota((SLOTS, 128), 0)
-        spread_rows = hot((iota((SLOTS, CHIPS), 0) >> 4) == iota((SLOTS, CHIPS), 1))
+        spread_rows = hot((iota((SLOTS, CHIPS), 0) >> 3) == iota((SLOTS, CHIPS), 1))
         picked = jnp.where(iota((SLOTS, 128), 1) == lane_of(row, ch, g), dot(spread_rows, requests()), 0.0)
         index = dot(picked.astype(BF16), jnp.ones((128, 128), BF16)).astype(jnp.int32)
         target = index + 256 * ((row & (MSG - 1)) >> 1)
         lane = iota((SLOTS, 128), 1)
-        pick = jnp.concatenate([hot(target == lane + 128 * b) for b in range(16)], axis=1)
+        pick = jnp.concatenate([hot(target == lane + 128 * b) for b in range(4 * PER)], axis=1)
         block = ag[pl.ds(PER * ch, PER)].reshape(PER * 2 * ROWS, WIDTH)
-        sb[ch] = dot(pick, block).astype(BF16).reshape(CHIPS, MSG, WIDTH)
-        spread(sb.at[ch], fet.at[ch], f_s.at[ch], f_r.at[ch])
-
-    shared = [0]
+        sb[ch] = stack(dot(pick, block))
+
+    def send_answer(ch, first, last):
+        spread(sb.at[ch], fet.at[ch], f_s.at[ch], f_r.at[ch], first, last)
+
+    def shares_landed(ch):
+        for at in range(PER * ch, PER * ch + PER):
+            for p in range(2):
+                share(at, p).wait_recv()
+
     for hop in range(6):
         for p in range(2):
             for side in range(2):
@@ -172,23 +199,33 @@
                     if hop < 5 and p in parts(hop + 1, side):
                         ring(side, hop + 1, p).start()
                     share(at, p).start()
-        if hop % 2 == 1:
-            ch = hop // 2
-            if ch == 0:
+            if hop and p == 0:
+                shares_landed(hop - 1)
+                answer(hop - 1)
+                send_answer(hop - 1, 1, CHIPS // 2)
+            elif hop:
+                send_answer(hop - 1, CHIPS // 2, CHIPS)
+            elif p:
                 landed(req, q_s)
                 landed(rq, q_r)
-            for at in range(PER * ch, PER * ch + PER):
-                for p in range(2):
-                    share(at, p).wait_recv()
-            answer(ch)
-
-    slot_c = event_slot(evc[...], g)
-    slot_r = event_slot(evr[...], g)
+    shares_landed(5)
+    answer(5)
+    send_answer(5, 1, CHIPS)
+
+    slot_r = event_slot(evs[...], g)
+    slot_c = []
+    for s in range(SEQS):
+        digits = jnp.where(iota((16, LEN), 0) == 0, slot_r[s : s + 1] >> 8, 0)
+        digits = jnp.where(iota((16, LEN), 0) == 1, slot_r[s : s + 1] & 255, digits)
+        worth = jnp.where(iota((16, 128), 0) == 0, 256.0, 1.0).astype(BF16)
+        slot_c.append(dot(digits.astype(F32).astype(BF16), worth, 0, 0).astype(jnp.int32))
+    slot_c = jnp.concatenate(slot_c, axis=0)
     x = jnp.zeros((EVENTS, WIDTH), F32)
     for ch in range(CHUNKS):
         landed(fet.at[ch], f_r.at[ch])
-        x += dot(hot(slot_c - SLOTS * ch == iota((EVENTS, SLOTS), 1)), fet[ch].reshape(SLOTS, WIDTH))
-    for load in loads:
+        where = [hot(slot_c - SLOTS * ch - 128 * b == iota((EVENTS, 128), 1)) for b in range(SLOTS // 128)]
+        x += dot(jnp.concatenate(where, axis=1), unstack(fet[ch]))
+    for load in loads[1:]:
         load.wait()
 
     xhat, xrstd = norm_stats(x)
@@ -245,9 +282,14 @@
     dx = cot[...].astype(F32) + norm_back(dnormed.astype(BF16).astype(F32), xhat_s[...], xrstd)
     high = dx.astype(BF16)
     low = (dx - high.astype(F32)).astype(BF16)
-    for ch in reversed(range(CHUNKS)):
-        where = hot(slot_r - SLOTS * ch == iota((SLOTS, EVENTS), 0))
-        sg[ch] = (dot(where, high) + dot(where, low)).astype(BF16).reshape(CHIPS, MSG, WIDTH)
+
+    def send_grads(ch):
+        total = jnp.zeros((SLOTS, WIDTH), F32)
+        for s in range(SEQS):
+            where = hot(slot_r[s : s + 1] - SLOTS * ch == iota((SLOTS, LEN), 0))
+            rows = slice(s * LEN, (s + 1) * LEN)
+            total += dot(where, high[rows]) + dot(where, low[rows])
+        sg[ch] = stack(total)
         spread(sg.at[ch], ret.at[ch], b_s.at[ch], b_r.at[ch])
 
     def swap(at):
@@ -257,11 +299,11 @@
         landed(ret.at[ch], b_r.at[ch])
         lane, col = iota((128, SLOTS), 0), iota((128, SLOTS), 1)
         sel = dot(requests(), hot(lane == lane_of(col, ch, g)))
-        mine = (iota((CHIPS, SLOTS), 1) >> 4) == iota((CHIPS, SLOTS), 0)
+        mine = (iota((CHIPS, SLOTS), 1) >> 3) == iota((CHIPS, SLOTS), 0)
         index = dot(jnp.ones((8, CHIPS), BF16), jnp.where(mine, sel, 0.0).astype(BF16))[0:1].astype(jnp.int32)
         kind = (iota((1, SLOTS), 1) & (MSG - 1)) >> 1
         row = iota((ROWS, SLOTS), 0)
-        grads = ret[ch].reshape(SLOTS, WIDTH)
+        grads = unstack(ret[ch])
         for j in reversed(range(PER)):
             at = PER * ch + j
             for other in (True, False):
@@ -281,13 +323,14 @@
             rs_s.at[side, 6 - s, p], rs_r.at[side, 6 - s, p], (nxt[side], l),
         )
 
-    done, got = [], []
+    for ch in reversed(range(CHUNKS)):
+        send_grads(ch)
+    got = []
     for s in range(6, -1, -1):
+        if s:
+            collect(s - 1)
         for side in range(2):
             at = place(s if side == 0 else -s)
-            if at // PER not in done:
-                collect(at // PER)
-                done.append(at // PER)
             if at not in got:
                 swap(at).wait_recv()
                 got.append(at)
@@ -326,8 +369,6 @@
 
 
 def local(table, projection_weight, output_weight, offsets, events, cotangent):
-    asked = offsets.reshape(GROUPS, CHIPS, 4).transpose(1, 0, 2).reshape(CHIPS, 1, 4 * GROUPS)
-    asked = jnp.pad(asked, ((0, 0), (0, 0), (0, 128 - 4 * GROUPS)))
     vmem, anym = pl.BlockSpec(memory_space=pltpu.VMEM), pl.BlockSpec(memory_space=pl.ANY)
     dma = pltpu.SemaphoreType.DMA
     out, grad = pl.pallas_call(
@@ -336,19 +377,21 @@
             jax.ShapeDtypeStruct((EVENTS, WIDTH), BF16),
             jax.ShapeDtypeStruct((ROWS, WIDTH), F32),
         ),
-        in_specs=[vmem] * 4 + [anym] * 3,
+        in_specs=[anym, vmem, vmem] + [anym] * 3,
         out_specs=(vmem, vmem),
         scratch_shapes=[
+            pltpu.VMEM((ROWS, WIDTH), F32),
             pltpu.VMEM((WIDTH, 4 * WIDTH), BF16),
             pltpu.VMEM((WIDTH, WIDTH), BF16),
             pltpu.VMEM((EVENTS, WIDTH), BF16),
-            dma((3,)),
+            dma((4,)),
             pltpu.VMEM((GROUPS, 2, ROWS, WIDTH), BF16),
-            pltpu.VMEM((CHIPS, 1, 128), jnp.int32),
-            pltpu.VMEM((CHUNKS, CHIPS, MSG, WIDTH), BF16),
-            pltpu.VMEM((CHUNKS, CHIPS, MSG, WIDTH), BF16),
-            pltpu.VMEM((CHUNKS, CHIPS, MSG, WIDTH), BF16),
-            pltpu.VMEM((CHUNKS, CHIPS, MSG, WIDTH), BF16),
+            pltpu.VMEM((CHIPS, 1, 128), F32),
+            pltpu.VMEM((CHIPS, 1, 128), F32),
+            pltpu.VMEM((CHUNKS, CHIPS, 2 * MSG, SIDE), BF16),
+            pltpu.VMEM((CHUNKS, CHIPS, 2 * MSG, SIDE), BF16),
+            pltpu.VMEM((CHUNKS, CHIPS, 2 * MSG, SIDE), BF16),
+            pltpu.VMEM((CHUNKS, CHIPS, 2 * MSG, SIDE), BF16),
             pltpu.VMEM((GROUPS, ROWS, WIDTH), F32),
             pltpu.VMEM((GROUPS, ROWS, WIDTH), BF16),
             pltpu.VMEM((GROUPS, ROWS, WIDTH), BF16),
@@ -368,9 +411,8 @@
         ),
     )(
         table,
-        asked,
-        events.reshape(EVENTS, 1),
-        events.reshape(1, EVENTS),
+        offsets[0].T,
+        events,
         cotangent.reshape(EVENTS, WIDTH),
         projection_weight,
         output_weight,

time: 151 us -> 134 us (0.89)
  Pallas kernels: 142 us -> 130 us
  local copies, waits for them, and re-layouts: 8.34 us -> 3.61 us
    pallas_call x1, Pallas kernels: 142 us -> 130 us  [local(): pl.pallas_call(kernel, out_shape=(jax.ShapeDtypeStruct((EVENTS, WIDTH), B...]
    reshape x4 -> x0, local copies, waits for them, and re-layouts: 3.09 us -> none  [the longest x1 1.56 us: local(): events.reshape(EVENTS, 1)]
    unnamed x3 -> x2, local copies, waits for them, and re-layouts: 4.48 us -> 3.61 us
where the time goes in v2:
time: 134 us
  Pallas kernels  130 us (97%)
  local copies, waits for them, and re-layouts  3.61 us (3%)
    pallas_call x1, Pallas kernels, local(): pl.pallas_call(kernel, out_shape=(jax.ShapeDtypeStruct((EVENTS, WIDTH), B...  130 us
    unnamed x2, local copies, waits for them, and re-layouts  3.61 us

profile of v2, /device:TPU:1, one launch (start us, length us, event | category | flops | bytes accessed | tf_op | source)
XLA Modules:
  0.0 133.9 jit_solution(14495946871488239938)
XLA Ops:
  0.6 129.7 %shard_map.77 = (bf16[352,512]{1,0:T(8,128)(2,1)}, f32[256,512]{1,0:T(8,128)}) custom-call(f32[256,512]{1,0:T(8,128)} %table_h.1, s32[2,768]{1,0:T(2,128)} %bitcast.7, s32[2,176]{1,0:T(2,128)} %evs.1, bf16[352,512]{1,0:T(8,128)(2,1)} %bitcast.6, bf16[512,2048]{1,0:T(8,128)(2,1)} %wp_h.1, bf16[512,512]{1,0:T(8,128)(2,1)} %wo_h.1), custom_call_target="tpu_custom_call" | custom-call | tf_op jit(solution)/shard_map/pallas_call | solution.py:374
  130.3 1.7 %copy.10 = bf16[2,176,512]{2,1,0:T(8,128)(2,1)} copy(bf16[2,176,512]{2,1,0:T(8,128)(2,1)} %bitcast.5) | data formatting | bytes 720896
  132.0 1.9 %copy.11 = f32[256,512]{1,0:T(8,128)} copy(f32[256,512]{1,0:T(8,128)} %get-tuple-element.9) | data formatting | bytes 1048576
